TPU v7x, 512 devices: a whole 4x8x8 slice. The times are simulated.
512 devices in a mesh: outer: 16 (over y, core), inner: 8 (over z), region: 4 (over x).
Axes of the slice: x: 4, y: 8, z: 8, core: 2. Of those that a mesh axis runs over, the one named last changes fastest.
Arguments:
- observations: float32 [1024, 128], P(('region', 'outer', 'inner')), parts along dimension 0, may hold values from -6 to 6
- obs_mask: int32 [1024, 128], P(('region', 'outer', 'inner')), parts along dimension 0, may hold values 0 or 1
- sensor_map: int32 [512], P('region'), parts along dimension 0, may hold values from 0 to 127
- transition: float32 [128, 128], replicated, may hold values from -1 to 1
- proc_noise: float32 [128, 128], replicated, may hold values from -1 to 1, as said below
- obs_var: float32 [128], replicated, may hold values from 0.1 to 1
- prior_mean: float32 [512], P('region'), parts along dimension 0, may hold values from -6 to 6
- prior_var: float32 [512], P('region'), parts along dimension 0, may hold values from 0.5 to 4
Outputs:
- filt_mean: float32 [1024, 128], P(('region', 'outer', 'inner')), parts along dimension 0
- filt_cov: float32 [1024, 128, 128], P(('region', 'outer', 'inner')), parts along dimension 0
There are 4 independent parts, one for each index of `region`. A program takes and returns all parts, laid end to end along the dimension named above; an argument that names none is the same for every part. Nothing has to cross between parts.
Inputs may be any that keep to these rules, and one draw needn't show every extreme that they name: `proc_noise`: symmetric positive definite.
All inputs are finite; a program needn't handle non-finite values. No bound on the sum of `obs_mask` on one device may be relied on, other than what follows from the above.
Results may differ from a plain program's by a relative error of at most 0.00017.
Values sent between devices are 32-bit elements; how exact they have to be, the bound alone decides.
A program may use at most 128 MiB of HBM per device.

v0:
```python
import jax
import jax.numpy as jnp
from jax import lax
from jax.sharding import Mesh
from jax.sharding import PartitionSpec as P

OUTER = ("outer_0", "outer_1")
OUTER_INNER = ("outer_0", "outer_1", "inner")
REGION_OUTER_INNER = ("region", "outer_0", "outer_1", "inner")


def neutral_like(value, identity):
    return jax.tree.map(
        lambda part, zero: jnp.zeros_like(part) + jnp.asarray(zero, part.dtype), value, identity
    )


def collected_together(value, axis):
    leaves = jax.tree.leaves(value)
    turns = sorted(range(len(leaves)), key=lambda k: -leaves[k].size)
    width = (1, *leaves[turns[0]].shape)[-1]
    lines = [
        jnp.pad(leaves[k].reshape(-1), (0, -leaves[k].size % width)).reshape(-1, width)
        for k in turns
    ]
    both, at, found = (lax.all_gather(jnp.concatenate(lines), axis), 0, {})
    for k, line in zip(turns, lines):
        section = both[:, at : at + len(line)].reshape(len(both), -1)
        found[k] = section[:, : leaves[k].size].reshape(-1, *leaves[k].shape)
        at += len(line)
    numbers = iter(range(len(leaves)))
    return jax.tree.map(lambda _: found[next(numbers)], value)


def gathered_by_type(value, axis):
    leaves, found = (jax.tree.leaves(value), {})
    for first, a in enumerate(leaves):
        if first not in found:
            alike = [k for k, b in enumerate(leaves) if b.dtype == a.dtype]
            got = (
                collected_together([leaves[k] for k in alike], axis)
                if len(alike) > 1
                else [lax.all_gather(a, axis)]
            )
            for k, b in zip(alike, got):
                found[k] = b
    numbers = iter(range(len(leaves)))
    return jax.tree.map(lambda _: found[next(numbers)], value)


def entering(value, axes, combine, identity):
    before = start = neutral_like(value, identity)
    running = value
    for axis in reversed(axes):
        devices, position = (lax.axis_size(axis), lax.axis_index(axis))
        pieces = gathered_by_type(running, axis)
        inside, running = (start, start)
        for k in range(devices):
            passed = k < position
            running = combine(running, jax.tree.map(lambda part: part[k], pieces))
            inside = jax.tree.map(lambda new, old: jnp.where(passed, new, old), running, inside)
        before = combine(inside, before)
    return before


def highest(left, right):
    return jnp.dot(left, right, precision=lax.Precision.HIGHEST)


def filter_step(carried, inputs, transition, proc_noise, sensor_map, obs_var):
    prev_mean, prev_cov = carried
    observed, mask_row = inputs
    weights = mask_row.astype(jnp.float32)
    pred_mean = highest(transition, prev_mean)
    pred_cov = highest(highest(transition, prev_cov), transition.T) + proc_noise
    picked = pred_cov[sensor_map] * weights[:, None]
    innov_cov = picked[:, sensor_map] * weights[None, :] + jnp.diag(obs_var)
    factor = jnp.linalg.cholesky(innov_cov)
    solved = jax.scipy.linalg.cho_solve((factor, True), picked)
    innovation = weights * (observed - pred_mean[sensor_map])
    new_mean = pred_mean + highest(solved.T, innovation)
    new_cov = pred_cov - highest(picked.T, solved)
    new_cov = 0.5 * (new_cov + new_cov.T)
    return ((new_mean, new_cov), (new_mean, new_cov))


def step_element(transition, proc_noise, sensor_map, obs_var, observed, mask_row):
    weights = mask_row.astype(jnp.float32)
    noise_rows = proc_noise[sensor_map] * weights[:, None]
    trans_rows = transition[sensor_map] * weights[:, None]
    innov_cov = noise_rows[:, sensor_map] * weights[None, :] + jnp.diag(obs_var)
    factor = jnp.linalg.cholesky(innov_cov)
    solved = jax.scipy.linalg.cho_solve((factor, True), noise_rows)
    masked_obs = weights * observed
    jump = transition - highest(solved.T, trans_rows)
    spread = proc_noise - highest(noise_rows.T, solved)
    spread = 0.5 * (spread + spread.T)
    offset = highest(solved.T, masked_obs)
    whitened = jax.scipy.linalg.solve_triangular(factor, trans_rows, lower=True)
    white_obs = jax.scipy.linalg.solve_triangular(factor, masked_obs, lower=True)
    info_vec = highest(whitened.T, white_obs)
    info_mat = highest(whitened.T, whitened)
    return (
        jnp.stack([jump, spread, info_mat]),
        jnp.stack([offset, info_vec]),
        jnp.ones((), jnp.float32),
    )


def first_element(
    transition, proc_noise, sensor_map, obs_var, prior_mean, prior_var, observed, mask_row
):
    start_state = (prior_mean, jnp.diag(prior_var))
    new_state, dropped = filter_step(
        start_state, (observed, mask_row), transition, proc_noise, sensor_map, obs_var
    )
    zero_mat = jnp.zeros_like(transition)
    zero_vec = jnp.zeros_like(prior_mean)
    return (
        jnp.stack([zero_mat, new_state[1], zero_mat]),
        jnp.stack([new_state[0], zero_vec]),
        jnp.ones((), jnp.float32),
    )


def blend_parts(early_spread, early_live, late_info):
    ident_mat = jnp.eye(early_spread.shape[0], dtype=jnp.float32)
    spread_root = jnp.linalg.cholesky(early_spread + (1.0 - early_live) * ident_mat)
    core = ident_mat + highest(spread_root.T, highest(late_info, spread_root))
    core = 0.5 * (core + core.T)
    core_root = jnp.linalg.cholesky(core)
    reduced = jax.scipy.linalg.solve_triangular(core_root, spread_root.T, lower=True)
    blended = highest(reduced.T, reduced)
    return (ident_mat, blended)


def combine(earlier, later):
    early_mats, early_vecs, early_live = earlier
    late_mats, late_vecs, late_live = later
    early_jump, early_spread, early_info = (early_mats[0], early_mats[1], early_mats[2])
    late_jump, late_spread, late_info = (late_mats[0], late_mats[1], late_mats[2])
    early_offset, early_vec = (early_vecs[0], early_vecs[1])
    late_offset, late_vec = (late_vecs[0], late_vecs[1])
    ident_mat, blended = blend_parts(early_spread, early_live, late_info)
    correction = ident_mat - highest(blended, late_info)
    moved = highest(correction, early_jump)
    jump = highest(late_jump, moved)
    offset = (
        highest(late_jump, highest(correction, early_offset) + highest(blended, late_vec))
        + late_offset
    )
    spread = highest(highest(late_jump, blended), late_jump.T) + late_spread
    spread = 0.5 * (spread + spread.T)
    info_mat = highest(moved.T, highest(late_info, early_jump)) + early_info
    info_mat = 0.5 * (info_mat + info_mat.T)
    info_vec = (
        highest(early_jump.T, highest(correction.T, late_vec - highest(late_info, early_offset)))
        + early_vec
    )
    joined = (
        jnp.stack([jump, spread, info_mat]),
        jnp.stack([offset, info_vec]),
        jnp.maximum(early_live, late_live),
    )
    keep_late = jax.tree.map(
        lambda joined_leaf, other_leaf: jnp.where(late_live > 0.5, joined_leaf, other_leaf),
        joined,
        earlier,
    )
    return jax.tree.map(
        lambda joined_leaf, other_leaf: jnp.where(early_live > 0.5, joined_leaf, other_leaf),
        keep_late,
        later,
    )


def local(
    observations, obs_mask, sensor_map, transition, proc_noise, obs_var, prior_mean, prior_var
):
    steps_here = observations.shape[0]
    state_dim = transition.shape[0]
    position = lax.axis_index(OUTER) * lax.axis_size("inner") + lax.axis_index("inner")

    def generic_at(counter):
        observed = lax.dynamic_index_in_dim(observations, counter, 0, keepdims=False)
        mask_row = lax.dynamic_index_in_dim(obs_mask, counter, 0, keepdims=False)
        return step_element(transition, proc_noise, sensor_map, obs_var, observed, mask_row)

    first_piece = lax.cond(
        position == 0,
        lambda: first_element(
            transition,
            proc_noise,
            sensor_map,
            obs_var,
            prior_mean,
            prior_var,
            observations[0],
            obs_mask[0],
        ),
        lambda: generic_at(0),
    )

    def fold_step(counter, carried):
        return combine(carried, generic_at(counter))

    own_element = lax.fori_loop(1, steps_here, fold_step, first_piece)
    zero_mat = jnp.zeros((state_dim, state_dim), jnp.float32)
    identity_el = (
        jnp.stack([jnp.eye(state_dim, dtype=jnp.float32), zero_mat, zero_mat]),
        jnp.zeros((2, state_dim), jnp.float32),
        jnp.zeros((), jnp.float32),
    )
    prior_cov = jnp.diag(prior_var)
    prefix = entering(own_element, OUTER_INNER, combine, identity_el)
    start_mean = jnp.where(prefix[2] > 0.5, prefix[1][0], prior_mean)
    start_cov = jnp.where(prefix[2] > 0.5, prefix[0][1], prior_cov)

    def advance(carried, inputs):
        return filter_step(carried, inputs, transition, proc_noise, sensor_map, obs_var)

    last_state, outputs = lax.scan(advance, (start_mean, start_cov), (observations, obs_mask))
    return (outputs[0], outputs[1])


def solution(mesh):
    finer = Mesh(
        mesh.devices.reshape(8, 2, mesh.shape["inner"], mesh.shape["region"]),
        ("outer_0", "outer_1", "inner", "region"),
    )
    in_specs = (
        P(REGION_OUTER_INNER, None),
        P(REGION_OUTER_INNER, None),
        P("region"),
        P(),
        P(),
        P(),
        P("region"),
        P("region"),
    )
    out_specs = (P(REGION_OUTER_INNER, None), P(REGION_OUTER_INNER, None, None))
    return jax.shard_map(local, mesh=finer, in_specs=in_specs, out_specs=out_specs, check_vma=False)
```

profile of v0, /device:TPU:56, one launch (start us, length us, event | category | flops | bytes accessed | tf_op | source)
XLA Modules:
  0.0 1116.3 jit_solution(1999130084898775535)
XLA Ops:
  12.8 11.7 %cholesky.647 = f32[128,128]{1,0:T(8,128)S(1)} custom-call(f32[128,128]{1,0:T(8,128)S(1)} %fusion.586), custom_call_target="Cholesky" | custom-call | tf_op jit(solution)/shard_map/while/body/eval_jaxpr/jit(cholesky)/cholesky | solution.py:92
  37.0 37.3 %conditional.1 = (f32[3,128,128]{2,1,0:T(8,128)S(1)}, f32[]{:T(128)}, f32[128]{0:T(128)S(1)}, f32[128]{0:T(128)S(1)}) conditional(s32[]{:T(128)} %convert_element_type.269, (s32[128]{0:T(128)S(1)}, f32[128,128]{1,0:T(8,128)S(1)}, s32[2,128]{1,0:T(2,128)S(1)}, f32[128]{0:T(128)S(1)}, f32[128,128]{1,0:T(8,128)S(1)}, ...), branch_computations={%region_0.7_spmd, %region_3.8_spmd} | conditional | flops 152078464 | bytes 3621418 | solution.py:189
  39.7 11.7 %cholesky.614 = f32[128,128]{1,0:T(8,128)S(1)} custom-call(f32[128,128]{1,0:T(8,128)S(1)} %fusion.13), custom_call_target="Cholesky" | custom-call | tf_op jit(solution)/shard_map/cond/branch_0_fun/jit(cholesky)/cholesky | solution.py:92
  76.2 11.7 %cholesky.658 = f32[128,128]{1,0:T(8,128)S(1)} custom-call(f32[128,128]{1,0:T(8,128)S(1)} %fusion.578), custom_call_target="Cholesky" | custom-call | tf_op jit(solution)/shard_map/while/body/eval_jaxpr/jit(cholesky)/cholesky | solution.py:128
  90.6 11.7 %cholesky.669 = f32[128,128]{1,0:T(8,128)S(1)} custom-call(f32[128,128]{1,0:T(8,128)S(1)} %fusion.577), custom_call_target="Cholesky" | custom-call | tf_op jit(solution)/shard_map/while/body/eval_jaxpr/jit(cholesky)/cholesky | solution.py:131
  119.3 47.6 %all-gather.9.cloned.1.call-done = f32[8,387,128]{2,1,0:T(8,128)} async-done(((f32[1,387,128]{2,1,0:T(8,128)}), f32[8,387,128]{2,1,0:T(8,128)}) %all-gather.9.cloned.1.call-update) | async-done | bytes 1585168 | tf_op jit(solution)/shard_map/all_gather | solution.py:26
  186.6 11.7 %cholesky.680 = f32[128,128]{1,0:T(8,128)S(1)} custom-call(f32[128,128]{1,0:T(8,128)S(1)} %fusion.559), custom_call_target="Cholesky" | custom-call | tf_op jit(solution)/shard_map/jit(cholesky)/cholesky | solution.py:128
  202.0 11.7 %cholesky.691 = f32[128,128]{1,0:T(8,128)S(1)} custom-call(f32[128,128]{1,0:T(8,128)S(1)} %fusion.558), custom_call_target="Cholesky" | custom-call | tf_op jit(solution)/shard_map/jit(cholesky)/cholesky | solution.py:131
  235.9 11.7 %cholesky.702 = f32[128,128]{1,0:T(8,128)S(1)} custom-call(f32[128,128]{1,0:T(8,128)S(1)} %fusion.546), custom_call_target="Cholesky" | custom-call | tf_op jit(solution)/shard_map/jit(cholesky)/cholesky | solution.py:128
  250.4 11.7 %cholesky.713 = f32[128,128]{1,0:T(8,128)S(1)} custom-call(f32[128,128]{1,0:T(8,128)S(1)} %fusion.545), custom_call_target="Cholesky" | custom-call | tf_op jit(solution)/shard_map/jit(cholesky)/cholesky | solution.py:131
  282.6 11.7 %cholesky.724 = f32[128,128]{1,0:T(8,128)S(1)} custom-call(f32[128,128]{1,0:T(8,128)S(1)} %fusion.533), custom_call_target="Cholesky" | custom-call | tf_op jit(solution)/shard_map/jit(cholesky)/cholesky | solution.py:128
  297.0 11.7 %cholesky.735 = f32[128,128]{1,0:T(8,128)S(1)} custom-call(f32[128,128]{1,0:T(8,128)S(1)} %fusion.532), custom_call_target="Cholesky" | custom-call | tf_op jit(solution)/shard_map/jit(cholesky)/cholesky | solution.py:131
  310.1 10.2 custom-call.57
  329.1 11.7 %cholesky.746 = f32[128,128]{1,0:T(8,128)S(1)} custom-call(f32[128,128]{1,0:T(8,128)S(1)} %fusion.520), custom_call_target="Cholesky" | custom-call | tf_op jit(solution)/shard_map/jit(cholesky)/cholesky | solution.py:128
  343.5 11.7 %cholesky.757 = f32[128,128]{1,0:T(8,128)S(1)} custom-call(f32[128,128]{1,0:T(8,128)S(1)} %fusion.519), custom_call_target="Cholesky" | custom-call | tf_op jit(solution)/shard_map/jit(cholesky)/cholesky | solution.py:131
  375.3 11.7 %cholesky.768 = f32[128,128]{1,0:T(8,128)S(1)} custom-call(f32[128,128]{1,0:T(8,128)S(1)} %fusion.507), custom_call_target="Cholesky" | custom-call | tf_op jit(solution)/shard_map/jit(cholesky)/cholesky | solution.py:128
  389.7 11.7 %cholesky.779 = f32[128,128]{1,0:T(8,128)S(1)} custom-call(f32[128,128]{1,0:T(8,128)S(1)} %fusion.506), custom_call_target="Cholesky" | custom-call | tf_op jit(solution)/shard_map/jit(cholesky)/cholesky | solution.py:131
  421.6 11.7 %cholesky.790 = f32[128,128]{1,0:T(8,128)S(1)} custom-call(f32[128,128]{1,0:T(8,128)S(1)} %fusion.494), custom_call_target="Cholesky" | custom-call | tf_op jit(solution)/shard_map/jit(cholesky)/cholesky | solution.py:128
  436.0 11.7 %cholesky.801 = f32[128,128]{1,0:T(8,128)S(1)} custom-call(f32[128,128]{1,0:T(8,128)S(1)} %fusion.493), custom_call_target="Cholesky" | custom-call | tf_op jit(solution)/shard_map/jit(cholesky)/cholesky | solution.py:131
  449.1 10.2 custom-call.60
  468.7 11.7 %cholesky.812 = f32[128,128]{1,0:T(8,128)S(1)} custom-call(f32[128,128]{1,0:T(8,128)S(1)} %fusion.481), custom_call_target="Cholesky" | custom-call | tf_op jit(solution)/shard_map/jit(cholesky)/cholesky | solution.py:128
  487.2 12.5 %cholesky.823 = f32[128,128]{1,0:T(8,128)S(1)} custom-call(f32[128,128]{1,0:T(8,128)} %fusion.480), custom_call_target="Cholesky" | custom-call | tf_op jit(solution)/shard_map/jit(cholesky)/cholesky | solution.py:131
  501.9 10.8 custom-call.61
  539.1 11.7 %cholesky.834 = f32[128,128]{1,0:T(8,128)S(1)} custom-call(f32[128,128]{1,0:T(8,128)S(1)} %fusion.461), custom_call_target="Cholesky" | custom-call | tf_op jit(solution)/shard_map/jit(cholesky)/cholesky | solution.py:128
  553.7 11.7 %cholesky.845 = f32[128,128]{1,0:T(8,128)S(1)} custom-call(f32[128,128]{1,0:T(8,128)S(1)} %fusion.460), custom_call_target="Cholesky" | custom-call | tf_op jit(solution)/shard_map/jit(cholesky)/cholesky | solution.py:131
  584.7 11.7 %cholesky.856 = f32[128,128]{1,0:T(8,128)S(1)} custom-call(f32[128,128]{1,0:T(8,128)S(1)} %fusion.447), custom_call_target="Cholesky" | custom-call | tf_op jit(solution)/shard_map/jit(cholesky)/cholesky | solution.py:128
  599.1 11.7 %cholesky.867 = f32[128,128]{1,0:T(8,128)S(1)} custom-call(f32[128,128]{1,0:T(8,128)S(1)} %fusion.446), custom_call_target="Cholesky" | custom-call | tf_op jit(solution)/shard_map/jit(cholesky)/cholesky | solution.py:131
  646.3 11.7 %cholesky.878 = f32[128,128]{1,0:T(8,128)S(1)} custom-call(f32[128,128]{1,0:T(8,128)S(1)} %fusion.434), custom_call_target="Cholesky" | custom-call | tf_op jit(solution)/shard_map/jit(cholesky)/cholesky | solution.py:128
  661.6 11.7 %cholesky.889 = f32[128,128]{1,0:T(8,128)S(1)} custom-call(f32[128,128]{1,0:T(8,128)S(1)} %fusion.433), custom_call_target="Cholesky" | custom-call | tf_op jit(solution)/shard_map/jit(cholesky)/cholesky | solution.py:131
  695.3 11.7 %cholesky.900 = f32[128,128]{1,0:T(8,128)S(1)} custom-call(f32[128,128]{1,0:T(8,128)S(1)} %fusion.421), custom_call_target="Cholesky" | custom-call | tf_op jit(solution)/shard_map/jit(cholesky)/cholesky | solution.py:128
  709.5 11.7 %cholesky.911 = f32[128,128]{1,0:T(8,128)S(1)} custom-call(f32[128,128]{1,0:T(8,128)S(1)} %fusion.420), custom_call_target="Cholesky" | custom-call | tf_op jit(solution)/shard_map/jit(cholesky)/cholesky | solution.py:131
  738.1 11.7 %cholesky.922 = f32[128,128]{1,0:T(8,128)S(1)} custom-call(f32[128,128]{1,0:T(8,128)S(1)} %fusion.408), custom_call_target="Cholesky" | custom-call | tf_op jit(solution)/shard_map/jit(cholesky)/cholesky | solution.py:128
  752.5 11.7 %cholesky.933 = f32[128,128]{1,0:T(8,128)S(1)} custom-call(f32[128,128]{1,0:T(8,128)S(1)} %fusion.407), custom_call_target="Cholesky" | custom-call | tf_op jit(solution)/shard_map/jit(cholesky)/cholesky | solution.py:131
  780.7 11.7 %cholesky.944 = f32[128,128]{1,0:T(8,128)S(1)} custom-call(f32[128,128]{1,0:T(8,128)S(1)} %fusion.395), custom_call_target="Cholesky" | custom-call | tf_op jit(solution)/shard_map/jit(cholesky)/cholesky | solution.py:128
  795.2 11.7 %cholesky.955 = f32[128,128]{1,0:T(8,128)S(1)} custom-call(f32[128,128]{1,0:T(8,128)S(1)} %fusion.394), custom_call_target="Cholesky" | custom-call | tf_op jit(solution)/shard_map/jit(cholesky)/cholesky | solution.py:131
  823.5 11.7 %cholesky.966 = f32[128,128]{1,0:T(8,128)S(1)} custom-call(f32[128,128]{1,0:T(8,128)S(1)} %fusion.382), custom_call_target="Cholesky" | custom-call | tf_op jit(solution)/shard_map/jit(cholesky)/cholesky | solution.py:128
  838.0 11.7 %cholesky.977 = f32[128,128]{1,0:T(8,128)S(1)} custom-call(f32[128,128]{1,0:T(8,128)S(1)} %fusion.381), custom_call_target="Cholesky" | custom-call | tf_op jit(solution)/shard_map/jit(cholesky)/cholesky | solution.py:131
  866.5 11.7 %cholesky.988 = f32[128,128]{1,0:T(8,128)S(1)} custom-call(f32[128,128]{1,0:T(8,128)S(1)} %fusion.369), custom_call_target="Cholesky" | custom-call | tf_op jit(solution)/shard_map/jit(cholesky)/cholesky | solution.py:128
  881.5 12.5 %cholesky.999 = f32[128,128]{1,0:T(8,128)S(1)} custom-call(f32[128,128]{1,0:T(8,128)} %fusion.368), custom_call_target="Cholesky" | custom-call | tf_op jit(solution)/shard_map/jit(cholesky)/cholesky | solution.py:131
  896.1 10.8 custom-call.69
  917.9 11.7 %cholesky.1010 = f32[128,128]{1,0:T(8,128)S(1)} custom-call(f32[128,128]{1,0:T(8,128)S(1)} %fusion.356), custom_call_target="Cholesky" | custom-call | tf_op jit(solution)/shard_map/jit(cholesky)/cholesky | solution.py:128
  934.4 12.5 %cholesky.1021 = f32[128,128]{1,0:T(8,128)S(1)} custom-call(f32[128,128]{1,0:T(8,128)} %fusion.355), custom_call_target="Cholesky" | custom-call | tf_op jit(solution)/shard_map/jit(cholesky)/cholesky | solution.py:131
  971.7 13.2 %cholesky.1032 = f32[128,128]{1,0:T(8,128)} custom-call(f32[128,128]{1,0:T(8,128)} %fusion.343), custom_call_target="Cholesky" | custom-call | tf_op jit(solution)/shard_map/jit(cholesky)/cholesky | solution.py:128
  996.5 13.2 %cholesky.1043 = f32[128,128]{1,0:T(8,128)} custom-call(f32[128,128]{1,0:T(8,128)} %fusion.342), custom_call_target="Cholesky" | custom-call | tf_op jit(solution)/shard_map/jit(cholesky)/cholesky | solution.py:131
  1013.2 11.6 %custom-call.71 = f32[1,128,128]{1,2,0:T(8,128)} custom-call(f32[1,128,128]{2,1,0:T(8,128)} %fusion.249), custom_call_target="InvertDiagBlocksLowerTriangular" | custom-call | tf_op jit(solution)/shard_map/jit(_solve_triangular)/triangular_solve/custom-call.0 | solution.py:132
  1049.7 59.6 %while.3 = (s32[]{:T(128)}, f32[128]{0:T(128)S(1)}, f32[128,128]{1,0:T(8,128)S(1)}, f32[2,128]{1,0:T(2,128)}, f32[2,128,128]{2,1,0:T(8,128)}, /*index=5*/f32[128...) while((s32[]{:T(128)}, f32[128]{0:T(128)S(1)}, ...), condition=%wide.region_5.10_spmd.clone, body=%wide.region_4.9_spmd.sunk.clone | while | flops 126584960 | bytes 2835591 | solution.py:222
  1053.6 11.7 %cholesky.2299 = f32[128,128]{1,0:T(8,128)S(1)} custom-call(f32[128,128]{1,0:T(8,128)S(1)} %fusion.1467), custom_call_target="Cholesky" | custom-call | tf_op jit(solution)/shard_map/while/body/eval_jaxpr/jit(cholesky)/cholesky | solution.py:78
  1083.3 11.7 %cholesky.2299 = f32[128,128]{1,0:T(8,128)S(1)} custom-call(f32[128,128]{1,0:T(8,128)S(1)} %fusion.1467), custom_call_target="Cholesky" | custom-call | tf_op jit(solution)/shard_map/while/body/eval_jaxpr/jit(cholesky)/cholesky | solution.py:78
  (969 shorter events, 474.3 us)
Async XLA Ops:
  7.2 28.5 %copy-start.50 = (s32[2,128]{1,0:T(2,128)S(1)}, s32[2,128]{1,0:T(2,128)}, u32[]{:S(2)}) copy-start(s32[2,128]{1,0:T(2,128)} %param.20) | copy-start | bytes 3076
  7.2 29.2 %copy-start.1 = (f32[128,128]{1,0:T(8,128)S(1)}, f32[128,128]{1,0:T(8,128)}, u32[]{:S(2)}) copy-start(f32[128,128]{1,0:T(8,128)} %param.23) | copy-start | bytes 196612
  7.2 5.3 copy-start.49
  7.2 28.5 %copy-start.51 = (f32[2,128]{1,0:T(2,128)S(1)}, f32[2,128]{1,0:T(2,128)}, u32[]{:S(2)}) copy-start(f32[2,128]{1,0:T(2,128)} %param.19) | copy-start | bytes 3076
  7.2 159.7 %all-gather.9.cloned.1.call-start = ((), (), s32[]{:S(2)}) async-start(), calls=%async_computation | async-start | bytes 1806336 | tf_op jit(solution)/shard_map/all_gather | solution.py:26
  8.6 28.2 %copy-start = (f32[128,128]{1,0:T(8,128)S(1)}, f32[128,128]{1,0:T(8,128)}, u32[]{:S(2)}) copy-start(f32[128,128]{1,0:T(8,128)} %param.22) | copy-start | bytes 196612
  10.2 26.8 %copy-start.55 = (f32[128]{0:T(128)S(1)}, f32[128]{0:T(128)}, u32[]{:S(2)}) copy-start(f32[128]{0:T(128)} %param.26) | copy-start | bytes 1540
  10.2 26.8 %copy-start.57 = (f32[128]{0:T(128)S(1)}, f32[128]{0:T(128)}, u32[]{:S(2)}) copy-start(f32[128]{0:T(128)} %param.25) | copy-start | bytes 1540
  10.2 26.8 %copy-start.60 = (s32[128]{0:T(128)S(1)}, s32[128]{0:T(128)}, u32[]{:S(2)}) copy-start(s32[128]{0:T(128)} %param.21) | copy-start | bytes 1540
  119.2 508.0 %all-gather.11.cloned.1.call-start = ((), (), s32[]{:S(2)}) async-start(), calls=%async_computation.1 | async-start | bytes 1806336 | tf_op jit(solution)/shard_map/all_gather | solution.py:26
  166.9 59.2 %copy-start.2 = (f32[8,387,128]{2,1,0:T(8,128)S(1)}, f32[8,387,128]{2,1,0:T(8,128)}, u32[]{:S(2)}) copy-start(f32[8,387,128]{2,1,0:T(8,128)} %all-gather.9.cloned.1.call-done) | copy-start | bytes 4755460
  275.6 46.9 %copy-start.53 = (f32[1,128]{1,0:T(1,128)}, f32[1,128]{1,0:T(1,128)S(1)}, u32[]{:S(2)}) copy-start(f32[1,128]{1,0:T(1,128)S(1)} %fusion.187) | copy-start | bytes 1540
  276.0 46.5 %copy-start.54 = (f32[1,128]{1,0:T(1,128)}, f32[1,128]{1,0:T(1,128)S(1)}, u32[]{:S(2)}) copy-start(f32[1,128]{1,0:T(1,128)S(1)} %fusion.191) | copy-start | bytes 1540
  525.5 6.9 copy-start.41
  578.7 4.7 copy-start.42
  578.7 4.7 copy-start.44
  627.1 58.8 %copy-start.3 = (f32[8,387,128]{2,1,0:T(8,128)S(1)}, f32[8,387,128]{2,1,0:T(8,128)}, u32[]{:S(2)}) copy-start(f32[8,387,128]{2,1,0:T(8,128)} %all-gather.11.cloned.1.call-done) | copy-start | bytes 4755460
  685.9 4.6 copy-start.4
  690.5 3.4 copy-start.47
  734.0 4.0 copy-start.6
  734.3 15.5 %copy-start.24 = (f32[128,128]{0,1:T(8,128)}, f32[128,128]{0,1:T(8,128)S(1)}, u32[]{:S(2)}) copy-start(f32[128,128]{0,1:T(8,128)S(1)} %copy.907) | copy-start | bytes 196612
  776.6 4.0 copy-start.8
  776.9 15.5 %copy-start.26 = (f32[128,128]{0,1:T(8,128)}, f32[128,128]{0,1:T(8,128)S(1)}, u32[]{:S(2)}) copy-start(f32[128,128]{0,1:T(8,128)S(1)} %copy.916) | copy-start | bytes 196612
  819.4 3.6 copy-start.10
  819.8 3.3 copy-start.28
  862.4 3.6 copy-start.11
  880.8 35.4 %copy-start.19 = (f32[3,128,128]{1,2,0:T(8,128)S(1)}, f32[3,128,128]{1,2,0:T(8,128)}, u32[]{:S(2)}) copy-start(f32[3,128,128]{1,2,0:T(8,128)} %copy.948) | copy-start | bytes 589828
  908.1 6.9 copy-start.13
  908.4 6.6 copy-start.35
  959.6 6.9 copy-start.15
  959.9 6.6 copy-start.39
  968.6 62.5 %copy-start.5 = (f32[128,128]{1,0:T(8,128)S(1)}, f32[128,128]{1,0:T(8,128)}, u32[]{:S(2)}) copy-start(f32[128,128]{1,0:T(8,128)} %copy-done.4) | copy-start | bytes 196612
  969.5 64.5 %copy-start.7 = (f32[128,128]{1,0:T(8,128)S(1)}, f32[128,128]{1,0:T(8,128)}, u32[]{:S(2)}) copy-start(f32[128,128]{1,0:T(8,128)} %copy-done.6) | copy-start | bytes 196612
  984.9 52.1 %copy-start.9 = (f32[128,128]{1,0:T(8,128)S(1)}, f32[128,128]{1,0:T(8,128)}, u32[]{:S(2)}) copy-start(f32[128,128]{1,0:T(8,128)} %copy-done.8) | copy-start | bytes 196612
  1028.6 12.6 %copy-start.32 = (f32[128,128]{0,1:T(8,128)S(1)}, f32[128,128]{0,1:T(8,128)}, u32[]{:S(2)}) copy-start(f32[128,128]{0,1:T(8,128)} %copy-done.31) | copy-start | bytes 196612
  1028.6 13.0 %copy-start.30 = (f32[128,128]{1,0:T(8,128)S(1)}, f32[128,128]{1,0:T(8,128)}, u32[]{:S(2)}) copy-start(f32[128,128]{1,0:T(8,128)} %copy-done.29) | copy-start | bytes 196612
  1028.6 13.4 %copy-start.12 = (f32[128,128]{1,0:T(8,128)S(1)}, f32[128,128]{1,0:T(8,128)}, u32[]{:S(2)}) copy-start(f32[128,128]{1,0:T(8,128)} %copy-done.11) | copy-start | bytes 196612
  1028.6 13.9 %copy-start.36 = (f32[128,128]{0,1:T(8,128)S(1)}, f32[128,128]{0,1:T(8,128)}, u32[]{:S(2)}) copy-start(f32[128,128]{0,1:T(8,128)} %copy-done.35) | copy-start | bytes 196612
  1028.7 14.3 %copy-start.34 = (f32[128,128]{1,0:T(8,128)S(1)}, f32[128,128]{1,0:T(8,128)}, u32[]{:S(2)}) copy-start(f32[128,128]{1,0:T(8,128)} %copy-done.33) | copy-start | bytes 196612
  1028.7 14.7 %copy-start.14 = (f32[128,128]{1,0:T(8,128)S(1)}, f32[128,128]{1,0:T(8,128)}, u32[]{:S(2)}) copy-start(f32[128,128]{1,0:T(8,128)} %copy-done.13) | copy-start | bytes 196612
  1028.7 15.2 %copy-start.40 = (f32[128,128]{0,1:T(8,128)S(1)}, f32[128,128]{0,1:T(8,128)}, u32[]{:S(2)}) copy-start(f32[128,128]{0,1:T(8,128)} %copy-done.39) | copy-start | bytes 196612
  1028.7 15.5 %copy-start.38 = (f32[128,128]{1,0:T(8,128)S(1)}, f32[128,128]{1,0:T(8,128)}, u32[]{:S(2)}) copy-start(f32[128,128]{1,0:T(8,128)} %copy-done.37) | copy-start | bytes 196612
  1031.3 13.7 %copy-start.16 = (f32[128,128]{1,0:T(8,128)S(1)}, f32[128,128]{1,0:T(8,128)}, u32[]{:S(2)}) copy-start(f32[128,128]{1,0:T(8,128)} %copy-done.15) | copy-start | bytes 196612
  1034.0 10.6 copy-start.45
  1034.2 13.5 %copy-start.18 = (f32[128,128]{1,0:T(8,128)S(1)}, f32[128,128]{1,0:T(8,128)}, u32[]{:S(2)}) copy-start(f32[128,128]{1,0:T(8,128)} %copy-done.17) | copy-start | bytes 196612
  1041.4 8.1 copy-start.58
  1041.4 8.1 copy-start.56
  1043.1 6.5 copy-start.61
  (16 other events, 18.6 us)
Sparse Core Ops, SparseCore 0:
  119.3 47.5 all-gather.8
  584.7 40.0 all-gather.10
where the time goes:
time: 1130 us; the launch traced here: 1120 us
  other arithmetic  784 us (69%)
  matrix products  146 us (13%)
  local copies, waits for them, and re-layouts  69.5 us (6%)
  between operations  57 us (5%)
  waiting for transfers between devices  47.6 us (4%)
    another operation x54, other arithmetic, blend_parts(): core_root = jnp.linalg.cholesky(core)  228 us
    another operation x54, other arithmetic, blend_parts(): jnp.linalg.cholesky(early_spread + (1.0 - early_live) * ident_mat)  226 us
    another operation x36, other arithmetic, blend_parts(): jax.scipy.linalg.solve_triangular(core_root, spread_root.T, lower=True)  197 us
    dot_general x308, matrix products, highest(): return jnp.dot(left, right, precision=lax.Precision.HIGHEST)  125 us
    all_gather x2, waiting for transfers between devices, collected_together(): both, at, found = (lax.all_gather(jnp.concatenate(lines), axis), 0, {})  47.6 us
    another operation x6, other arithmetic, filter_step(): factor = jnp.linalg.cholesky(innov_cov)  24.9 us
    another operation x6, other arithmetic, step_element(): factor = jnp.linalg.cholesky(innov_cov)  24.9 us
  transfers between devices with their start and end apart: 2, of which 1 were waited for; matrix products, arithmetic and copies ran while one was open for 4% of the time, Pallas kernels for 0%

commit v1 on v0

v1 whole, which is shorter than its diff:
```python
import functools

import jax
import jax.numpy as jnp
from jax import lax
from jax.experimental import pallas as pl
from jax.experimental.pallas import tpu as pltpu
from jax.sharding import PartitionSpec as P

N = 128
BF = jnp.bfloat16
F32 = jnp.float32
BLOCK = 32
NN = (((1,), (0,)), ((), ()))
NT = (((1,), (1,)), ((), ()))
TN = (((0,), (0,)), ((), ()))
MESH = pl.DeviceIdType.MESH


def dot(left, right, dims):
    return lax.dot_general(
        left, right, dims, precision=lax.Precision.HIGHEST, preferred_element_type=F32
    )


def iota(dim, shape=(N, N)):
    return lax.broadcasted_iota(jnp.int32, shape, dim)


def split3(x):
    high = x.astype(BF)
    rest = x - high.astype(F32)
    mid = rest.astype(BF)
    return high, mid, (rest - mid.astype(F32)).astype(BF)


def factor(S, tiles, floors=None, done=None):
    sub, lane = iota(0, (8, N)), iota(1, (8, N))
    groups = BLOCK // 8
    for row0 in range(0, N, BLOCK):
        panel = [
            [S[row0 + 8 * q : row0 + 8 * q + 8, N * c : N * c + N] for q in range(groups)]
            for c in range(tiles)
        ]
        cols = [
            [
                jnp.broadcast_to(panel[0][q][:, row0 + k : row0 + k + 1], (8, N))
                if q >= k // 8
                else None
                for q in range(groups)
            ]
            for k in range(BLOCK)
        ]
        scale = [jnp.zeros((8, N), F32) for _ in range(groups)]
        raised = [jnp.zeros((8, N), F32) for _ in range(groups)]
        for j in range(BLOCK):
            r, s = j // 8, j % 8
            pivot = jnp.broadcast_to(cols[j][r][s : s + 1, :], (8, N))
            if floors is not None:
                low = jnp.broadcast_to(floors[row0 // 8 + r][s : s + 1, :], (8, N))
                kept = jnp.maximum(pivot, low)
                raised[r] = jnp.where(sub == s, kept - pivot, raised[r])
                pivot = kept
            inverse, root = 1.0 / pivot, lax.rsqrt(pivot)
            scale[r] = jnp.where(sub == s, root, scale[r])
            mult = [cols[j][q] * inverse if q >= r else None for q in range(groups)]
            if s < 7:
                below = jnp.where(sub > s, mult[r], 0.0)
            for c in range(tiles):
                line = jnp.broadcast_to(panel[c][r][s : s + 1, :], (8, N))
                if s < 7:
                    panel[c][r] = panel[c][r] - below * line
                for q in range(r + 1, groups):
                    panel[c][q] = panel[c][q] - mult[q] * line
            for k in range(j + 1, BLOCK):
                line = jnp.broadcast_to(cols[j][k // 8][k % 8 : k % 8 + 1, :], (8, N))
                for q in range(k // 8, groups):
                    cols[k][q] = cols[k][q] - mult[q] * line
        for q in range(groups):
            if floors is not None:
                diagonal = lane == sub + (row0 + 8 * q)
                panel[0][q] = panel[0][q] + jnp.where(diagonal, raised[q], 0.0)
            for c in range(tiles):
                panel[c][q] = panel[c][q] * scale[q]
                S[row0 + 8 * q : row0 + 8 * q + 8, N * c : N * c + N] = panel[c][q]
        if done is not None:
            done(row0, panel[0])
        if row0 + BLOCK < N:
            row1 = row0 + BLOCK
            whole = jnp.concatenate(
                [jnp.concatenate([panel[c][q] for c in range(tiles)], axis=1) for q in range(groups)],
                axis=0,
            )
            h, m, l = split3(whole)
            right = jnp.concatenate([h, m, h, l, h, m], axis=0)
            h, m, l = h[:, :N], m[:, :N], l[:, :N]
            left = jnp.concatenate([h, h, m, h, l, m], axis=0)
            update = lax.dot_general(left, right, TN, preferred_element_type=F32)
            S[row1:, :] = S[row1:, :] - update[row1:, :]


def cholesky(S, C, out, sent=None):
    eye = iota(0) == iota(1)
    S[...] = C
    low = jnp.sum(jnp.where(eye, C, 0.0), axis=1, keepdims=True) * 2e-7 + 1e-30
    low = jnp.broadcast_to(low, (N, N))
    sub, lane = iota(0, (8, N)), iota(1, (8, N))

    def done(row0, lines):
        for q in range(BLOCK // 8):
            row = row0 + 8 * q
            out[row : row + 8, :] = jnp.where(lane >= sub + row, lines[q], 0.0)
        if sent is not None:
            sent(row0 // BLOCK)

    factor(S, 1, [low[8 * q : 8 * q + 8, :] for q in range(N // 8)], done)


def kernel(
    outer, inner,
    obs_ref, mask_ref, map_ref, F_ref, Q_ref, r_ref, pm_ref, pv_ref,
    mean_ref, cov_ref,
    oU, ob, oAJ, rU, rb, rAJ, C, S, SC, gzs, gzr,
    send_sem, recv_sem, gz_sem,
):
    devices = outer * inner
    levels = devices.bit_length() - 1
    me_o, me_i, me_r = lax.axis_index("outer"), lax.axis_index("inner"), lax.axis_index("region")
    d = me_o * inner + me_i

    def place(index):
        return (index // inner, index % inner, me_r)

    barrier = pltpu.get_barrier_semaphore()
    targets = jnp.int32(0)
    for k in range(levels):
        @pl.when(d >= 2**k)
        def _():
            pl.semaphore_signal(barrier, inc=1, device_id=place(d - 2**k), device_id_type=MESH)
        targets = targets + jnp.where(d + 2**k < devices, 1, 0)

    one_hot = jnp.where(iota(0) == jnp.broadcast_to(map_ref[...], (N, N)), 1.0, 0.0)
    weight = mask_ref[...].astype(F32) / r_ref[...]
    rows = jnp.concatenate([weight, weight * obs_ref[...], jnp.zeros((4, N), F32)], axis=0)
    gzs[...] = dot(rows, one_hot, NT)

    @pl.when(targets > 0)
    def _():
        pl.semaphore_wait(barrier, targets)

    def gz_copy(to):
        return pltpu.make_async_remote_copy(
            src_ref=gzs, dst_ref=gzr, send_sem=gz_sem.at[0], recv_sem=gz_sem.at[1],
            device_id=place(to), device_id_type=MESH,
        )

    @pl.when(d + 1 < devices)
    def _():
        gz_copy(d + 1).start()

    eye = iota(0) == iota(1)
    zero8 = jnp.zeros((8, N), F32)
    row8 = iota(0, (8, N))
    C[...] = Q_ref[...]
    ob[0] = zero8
    oAJ[0, 0:N, :] = F_ref[...]
    S[...] = jnp.zeros_like(S)
    prior = jnp.where(eye, jnp.broadcast_to(pv_ref[...], (N, N)), 0.0)
    cholesky(SC, jnp.where(d == 0, prior, Q_ref[...]), rU.at[0])

    @pl.when(d == 0)
    def _():
        oAJ[0, N:, :] = jnp.zeros((N + 8, N), F32)
        rb[0] = jnp.where(row8 == 0, jnp.broadcast_to(pm_ref[...], (8, N)), 0.0)

    @pl.when(d > 0)
    def _():
        gz_copy(d).wait_recv()
        for ref, step in ((rAJ, 0), (oAJ, 1)):
            g, z = gzr[step : step + 1, :], gzr[2 + step : 3 + step, :]
            ref[0, N : 2 * N, :] = jnp.where(eye, jnp.broadcast_to(g, (N, N)), 0.0)
            ref[0, 2 * N :, :] = jnp.where(row8 == 0, jnp.broadcast_to(z, (8, N)), 0.0)
        rAJ[0, 0:N, :] = F_ref[...]
        rb[0] = zero8

    def remote(source, target, slot, which, to):
        return pltpu.make_async_remote_copy(
            src_ref=source, dst_ref=target,
            send_sem=send_sem.at[slot, which], recv_sem=recv_sem.at[slot, which],
            device_id=place(to), device_id_type=MESH,
        )

    blocks = N // BLOCK

    def copy_U(slot, p, to):
        lines = pl.ds(p * BLOCK, BLOCK)
        return remote(oU.at[slot, lines], rU.at[slot, lines], slot, p, to)

    def copy_b(slot, to):
        return remote(ob.at[slot], rb.at[slot], slot, blocks, to)

    def copy_AJ(slot, to):
        return remote(oAJ.at[slot], rAJ.at[slot], slot, blocks + 1, to)

    def level(i, ahead):
        back = ahead // 2
        full = d >= ahead
        goes = d + ahead < devices

        @pl.when(d >= back)
        def _():
            @pl.when(i > 0)
            def _():
                copy_b(i, d).wait_recv()
                for p in range(blocks):
                    copy_U(i, p, d).wait_recv()

            U, b1, A2, eta2 = rU[i], rb[i], oAJ[i, 0:N, :], oAJ[i, 2 * N :, :]
            UJ = dot(U, oAJ[i, N : 2 * N, :], NT)
            S[:, 0:N] = dot(UJ, U, NT) + jnp.where(eye, 1.0, 0.0)
            S[:, N : 2 * N] = dot(U, A2, NT)
            S[:, 2 * N : 3 * N] = UJ
            S[:, 3 * N : 3 * N + 8] = dot(U, eta2, NT) - dot(UJ, b1, NT)
            factor(S, 4)
            KY = S[:, N : 2 * N]
            gram = dot(jnp.concatenate([KY, S[:, 3 * N :]], axis=1), KY, TN)
            new_C = C[...] + gram[0:N, :]
            C[...] = new_C
            ob[i + 1] = ob[i] + dot(b1, A2, NT) + gram[N : N + 8, :]

            @pl.when(goes)
            def _():
                copy_b(i + 1, d + ahead).start()
                cholesky(SC, new_C, oU.at[i + 1], lambda p: copy_U(i + 1, p, d + ahead).start())

        @pl.when(d < back)
        def _():
            oU[i + 1] = oU[i]
            ob[i + 1] = ob[i]

            @pl.when(goes)
            def _():
                copy_b(i + 1, d + ahead).start()
                for p in range(blocks):
                    copy_U(i + 1, p, d + ahead).start()

        @pl.when(full)
        def _():
            @pl.when(i > 0)
            def _():
                copy_AJ(i, d).wait_recv()

            A1, J2 = rAJ[i, 0:N, :], oAJ[i, N : 2 * N, :]
            q = oAJ[i, 2 * N :, :] - dot(rb[i], J2, NT)
            KR = dot(S[:, 2 * N : 3 * N], A1, NN)
            others = dot(jnp.concatenate([oAJ[i, 0 : 2 * N, :], q], axis=0), A1, NN)
            gram = dot(jnp.concatenate([KR, S[:, N : 2 * N], S[:, 3 * N :]], axis=1), KR, TN)
            moved = dot(A1, others[N : 2 * N, :], TN)
            oAJ[i + 1, 0:N, :] = others[0:N, :] - gram[N : 2 * N, :]
            oAJ[i + 1, N : 2 * N, :] = rAJ[i, N : 2 * N, :] + moved - gram[0:N, :]
            oAJ[i + 1, 2 * N :, :] = (
                rAJ[i, 2 * N :, :] + others[2 * N :, :] - gram[2 * N : 2 * N + 8, :]
            )

            @pl.when(goes)
            def _():
                copy_AJ(i + 1, d + ahead).start()

        return ahead * 2

    lax.fori_loop(0, levels + 1, level, jnp.int32(1))

    cov = C[...]
    mean = ob[levels + 1]
    for step in range(2):
        g, z = gzs[step : step + 1, :], gzs[2 + step : 3 + step, :]
        across = jnp.broadcast_to(jnp.sqrt(g), (N, N))
        down = across.T
        scaled = down * cov
        S[:, 0:N] = scaled * across + jnp.where(eye, 1.0, 0.0)
        S[:, N : 2 * N] = scaled
        if step == 0:
            cov_F = dot(cov, F_ref[...], NT)
            S[:, 2 * N : 3 * N] = down * cov_F
            spread = dot(F_ref[...], cov_F, NN)
            tiles = 3
        else:
            tiles = 2
        factor(S.at[:, 0 : tiles * N], tiles)
        K = S[:, N : 2 * N]
        new_cov = cov - dot(K, K, TN)
        new_cov = 0.5 * (new_cov + new_cov.T)
        cov_ref[step] = new_cov
        new_mean = mean + dot(z - g * mean, new_cov, NN)
        mean_ref[step : step + 1, :] = new_mean[0:1, :]
        if step == 0:
            K = S[:, 2 * N : 3 * N]
            cov = spread + Q_ref[...] - dot(K, K, TN)
            cov = 0.5 * (cov + cov.T)
            mean = dot(new_mean, F_ref[...], NT)

    @pl.when(d + 1 < devices)
    def _():
        gz_copy(d + 1).wait_send()

    def drain(i, ahead):
        @pl.when(d + ahead < devices)
        def _():
            copy_b(i + 1, d + ahead).wait_send()
            for p in range(blocks):
                copy_U(i + 1, p, d + ahead).wait_send()

            @pl.when(d >= ahead)
            def _():
                copy_AJ(i + 1, d + ahead).wait_send()

        return ahead * 2

    lax.fori_loop(0, levels, drain, jnp.int32(1))


def local(outer, inner, obs, mask, smap, F, Q, r, pm, pv):
    devices = outer * inner
    levels = devices.bit_length() - 1
    vmem = pl.BlockSpec(memory_space=pltpu.VMEM)
    slots = levels + 2
    return pl.pallas_call(
        functools.partial(kernel, outer, inner),
        out_shape=(
            jax.ShapeDtypeStruct((2, N), F32),
            jax.ShapeDtypeStruct((2, N, N), F32),
        ),
        in_specs=[vmem] * 8,
        out_specs=(vmem, vmem),
        scratch_shapes=[
            pltpu.VMEM((slots, N, N), F32),
            pltpu.VMEM((slots, 8, N), F32),
            pltpu.VMEM((slots, 2 * N + 8, N), F32),
            pltpu.VMEM((slots, N, N), F32),
            pltpu.VMEM((slots, 8, N), F32),
            pltpu.VMEM((slots, 2 * N + 8, N), F32),
            pltpu.VMEM((N, N), F32),
            pltpu.VMEM((N, 4 * N), F32),
            pltpu.VMEM((N, N), F32),
            pltpu.VMEM((8, N), F32),
            pltpu.VMEM((8, N), F32),
            pltpu.SemaphoreType.DMA((slots, N // BLOCK + 2)),
            pltpu.SemaphoreType.DMA((slots, N // BLOCK + 2)),
            pltpu.SemaphoreType.DMA((2,)),
        ],
        compiler_params=pltpu.CompilerParams(
            collective_id=0, has_side_effects=True, vmem_limit_bytes=48 * 1024 * 1024
        ),
    )(obs, mask, smap.reshape(1, N), F, Q, r.reshape(1, N), pm.reshape(1, N), pv.reshape(1, N))


def solution(mesh):
    outer, inner = mesh.shape["outer"], mesh.shape["inner"]
    split = P(("region", "outer", "inner"))
    return jax.shard_map(
        functools.partial(local, outer, inner),
        mesh=mesh,
        in_specs=(split, split, P("region"), P(), P(), P(), P("region"), P("region")),
        out_specs=(split, split),
        check_vma=False,
    )
```

time: 1130 us -> 106 us (0.09); the launches traced: 1120 us -> 105 us
  other arithmetic: 784 us -> 0 us
  matrix products: 146 us -> 0 us
  Pallas kernels: 0 us -> 101 us
  local copies, waits for them, and re-layouts: 69.5 us -> 3.59 us
  between operations: 57 us -> 0.69 us
  waiting for transfers between devices: 47.6 us -> 0 us
    another operation x211 -> x0, other arithmetic: 761 us -> none  [the longest x54 228 us: blend_parts(): core_root = jnp.linalg.cholesky(core)]
    dot_general x308 -> x0, matrix products: 125 us -> none  [highest(): return jnp.dot(left, right, precision=lax.Precision.HIGHEST)]
    pallas_call x0 -> x1, Pallas kernels: none -> 101 us  [local(): pl.pallas_call(functools.partial(kernel, outer, inner), out_shape=(jax.Sh...]
    all_gather x2 -> x0, waiting for transfers between devices: 47.6 us -> none  [collected_together(): both, at, found = (lax.all_gather(jnp.concatenate(lines), axis), 0, {})]
    another operation x30 -> x0, matrix products: 20.2 us -> none  [the longest x18 17.3 us: blend_parts(): jax.scipy.linalg.solve_triangular(core_root, spread_root.T, lower=True)]
    another operation x9 -> x0, local copies, waits for them, and re-layouts: 12.4 us -> none  [the longest x8 12.3 us: combine(): jnp.stack([jump, spread, info_mat])]
  transfers between devices with their start and end apart: 2 -> 0, of which waited for: 1 -> 0; matrix products, arithmetic and copies ran while one was open for 4% -> 0% of each run, Pallas kernels for 0% -> 0%
where the time goes in v1:
time: 106 us; the launch traced here: 105 us
  Pallas kernels  101 us (95%)
  local copies, waits for them, and re-layouts  3.59 us (3%)
    pallas_call x1, Pallas kernels, local(): pl.pallas_call(functools.partial(kernel, outer, inner), out_shape=(jax.Sh...  101 us
    unnamed x18, local copies, waits for them, and re-layouts  3.59 us

profile of v1, /device:TPU:56, one launch (start us, length us, event | category | flops | bytes accessed | tf_op | source)
XLA Modules:
  0.0 105.3 jit_solution(13454921041360847555)
XLA Ops:
  0.6 0.0 copy-start.7
  0.6 0.0 copy-start.3
  0.7 0.0 copy-start.5
  0.7 0.0 copy-start.6
  0.7 0.0 copy-start.2
  0.7 0.0 copy-start.4
  0.7 0.6 copy-done.7
  1.3 0.0 copy-done.3
  1.3 0.0 copy-done.5
  1.3 0.0 copy-done.6
  1.3 0.0 copy-done.2
  1.4 0.0 copy-done.4
  1.4 0.0 copy-start
  1.4 0.8 copy-done
  2.2 0.0 copy-start.1
  2.2 0.8 copy-done.1
  3.1 101.0 %shard_map.95 = (f32[2,128]{1,0:T(2,128)S(1)}, f32[2,128,128]{2,1,0:T(8,128)S(1)}) custom-call(f32[2,128]{1,0:T(2,128)S(1)} %copy-done.2, s32[2,128]{1,0:T(2,128)S(1)} %copy-done.3, s32[1,128]{1,0:T(1,128)S(1)} %bitcast.4, f32[128,128]{1,0:T(8,128)S(1)} %copy-done, f32[128,128]{1,0:T(8,128)S(1)} %copy-done.1, f32[1,128]{1,0:T(1,128)S(1)} %bitcast.5, ...), custom_call_target="tpu_custom_call" | custom-call | tf_op jit(solution)/shard_map/pallas_call | solution.py:327
  104.1 0.6 copy.12
  104.6 0.7 copy.13
Async XLA Ops:
  0.6 0.7 copy-start.7
  0.6 0.7 copy-start.3
  0.7 0.7 copy-start.5
  0.7 0.7 copy-start.6
  0.7 0.7 copy-start.2
  0.7 0.7 copy-start.4
  1.4 0.8 copy-start
  2.2 0.8 copy-start.1

commit v2 on v1

v2 whole, which is shorter than its diff:
```python
import functools

import jax
import jax.numpy as jnp
from jax import lax
from jax.experimental import pallas as pl
from jax.experimental.pallas import tpu as pltpu
from jax.sharding import PartitionSpec as P

N = 128
BF = jnp.bfloat16
F32 = jnp.float32
BLOCK = 32
NN = (((1,), (0,)), ((), ()))
NT = (((1,), (1,)), ((), ()))
TN = (((0,), (0,)), ((), ()))
MESH = pl.DeviceIdType.MESH


def dot(left, right, dims):
    return lax.dot_general(
        left, right, dims, precision=lax.Precision.HIGHEST, preferred_element_type=F32
    )


def iota(dim, shape=(N, N)):
    return lax.broadcasted_iota(jnp.int32, shape, dim)


def split3(x):
    high = x.astype(BF)
    rest = x - high.astype(F32)
    mid = rest.astype(BF)
    return high, mid, (rest - mid.astype(F32)).astype(BF)


def factor(*jobs):
    sub = iota(0, (8, N))
    groups = BLOCK // 8
    for row0 in range(0, N, BLOCK):
        work = []
        for S, tiles in jobs:
            panel = [
                [S[row0 + 8 * q : row0 + 8 * q + 8, N * c : N * c + N] for q in range(groups)]
                for c in range(tiles)
            ]
            cols = [
                [
                    jnp.broadcast_to(panel[0][q][:, row0 + k : row0 + k + 1], (8, N))
                    if q >= k // 8
                    else None
                    for q in range(groups)
                ]
                for k in range(BLOCK)
            ]
            scale = [jnp.zeros((8, N), F32) for _ in range(groups)]
            work.append((S, tiles, panel, cols, scale))
        for j in range(BLOCK):
            r, s = j // 8, j % 8
            for S, tiles, panel, cols, scale in work:
                pivot = jnp.broadcast_to(cols[j][r][s : s + 1, :], (8, N))
                inverse = 1.0 / pivot
                scale[r] = jnp.where(sub == s, lax.rsqrt(pivot), scale[r])
                mult = [cols[j][q] * inverse if q >= r else None for q in range(groups)]
                if s < 7:
                    below = jnp.where(sub > s, mult[r], 0.0)
                for k in range(j + 1, BLOCK):
                    line = jnp.broadcast_to(cols[j][k // 8][k % 8 : k % 8 + 1, :], (8, N))
                    for q in range(k // 8, groups):
                        cols[k][q] = cols[k][q] - mult[q] * line
                for c in range(tiles):
                    line = jnp.broadcast_to(panel[c][r][s : s + 1, :], (8, N))
                    if s < 7:
                        panel[c][r] = panel[c][r] - below * line
                    for q in range(r + 1, groups):
                        panel[c][q] = panel[c][q] - mult[q] * line
        for S, tiles, panel, cols, scale in work:
            for q in range(groups):
                for c in range(tiles):
                    panel[c][q] = panel[c][q] * scale[q]
                    S[row0 + 8 * q : row0 + 8 * q + 8, N * c : N * c + N] = panel[c][q]
        if row0 + BLOCK < N:
            row1 = row0 + BLOCK
            for S, tiles, panel, cols, scale in work:
                whole = jnp.concatenate(
                    [
                        jnp.concatenate([panel[c][q] for c in range(tiles)], axis=1)
                        for q in range(groups)
                    ],
                    axis=0,
                )
                h, m, l = split3(whole)
                right = jnp.concatenate([h, m, h, l, h, m], axis=0)
                h, m, l = h[:, :N], m[:, :N], l[:, :N]
                left = jnp.concatenate([h, h, m, h, l, m], axis=0)
                update = lax.dot_general(left, right, TN, preferred_element_type=F32)
                S[row1:, :] = S[row1:, :] - update[row1:, :]


def kernel(
    outer, inner,
    obs_ref, mask_ref, map_ref, F_ref, Q_ref, r_ref, pm_ref, pv_ref,
    mean_ref, cov_ref,
    oL, ob, oAJ, rL, rb, rAJ, B, M, S, T, gzs, gzr,
    send_sem, recv_sem, gz_sem,
):
    devices = outer * inner
    levels = devices.bit_length() - 1
    me_o, me_i, me_r = lax.axis_index("outer"), lax.axis_index("inner"), lax.axis_index("region")
    d = me_o * inner + me_i

    def place(index):
        return (index // inner, index % inner, me_r)

    barrier = pltpu.get_barrier_semaphore()
    targets = jnp.int32(0)
    for k in range(levels):
        @pl.when(d >= 2**k)
        def _():
            pl.semaphore_signal(barrier, inc=1, device_id=place(d - 2**k), device_id_type=MESH)
        targets = targets + jnp.where(d + 2**k < devices, 1, 0)

    one_hot = jnp.where(iota(0) == jnp.broadcast_to(map_ref[...], (N, N)), 1.0, 0.0)
    weight = mask_ref[...].astype(F32) / r_ref[...]
    rows = jnp.concatenate([weight, weight * obs_ref[...], jnp.zeros((4, N), F32)], axis=0)
    gzs[...] = dot(rows, one_hot, NT)

    @pl.when(targets > 0)
    def _():
        pl.semaphore_wait(barrier, targets)

    def gz_copy(to):
        return pltpu.make_async_remote_copy(
            src_ref=gzs, dst_ref=gzr, send_sem=gz_sem.at[0], recv_sem=gz_sem.at[1],
            device_id=place(to), device_id_type=MESH,
        )

    @pl.when(d + 1 < devices)
    def _():
        gz_copy(d + 1).start()

    eye = iota(0) == iota(1)
    zero8 = jnp.zeros((8, N), F32)
    row8 = iota(0, (8, N))
    ob[0] = zero8
    S[...] = jnp.zeros_like(S)
    unit = jnp.where(eye, 1.0, 0.0)
    F = F_ref[...]
    T[:, 0:N] = Q_ref[...]
    T[:, N:] = unit
    factor((T, 2))
    K = T[:, N:]
    inverse = dot(K, K, TN)
    oL[0] = inverse
    oAJ[0, 0:N, :] = F
    FL = dot(F, inverse, TN)
    B[...] = FL
    M[...] = dot(FL, F, NN)

    @pl.when(d == 0)
    def _():
        oAJ[0, N:, :] = jnp.zeros((N + 8, N), F32)
        rL[0] = jnp.where(eye, 1.0 / jnp.broadcast_to(pv_ref[...], (N, N)), 0.0)
        rb[0] = jnp.where(row8 == 0, jnp.broadcast_to(pm_ref[...], (8, N)), 0.0)

    @pl.when(d > 0)
    def _():
        gz_copy(d).wait_recv()
        for ref, step in ((rAJ, 0), (oAJ, 1)):
            g, z = gzr[step : step + 1, :], gzr[2 + step : 3 + step, :]
            ref[0, N : 2 * N, :] = jnp.where(eye, jnp.broadcast_to(g, (N, N)), 0.0)
            ref[0, 2 * N :, :] = jnp.where(row8 == 0, jnp.broadcast_to(z, (8, N)), 0.0)
        rAJ[0, 0:N, :] = F
        rL[0] = inverse
        rb[0] = zero8

    def remote(source, target, slot, which, to):
        return pltpu.make_async_remote_copy(
            src_ref=source, dst_ref=target,
            send_sem=send_sem.at[slot, which], recv_sem=recv_sem.at[slot, which],
            device_id=place(to), device_id_type=MESH,
        )

    def copy_L(slot, to):
        return remote(oL.at[slot], rL.at[slot], slot, 0, to)

    def copy_b(slot, to):
        return remote(ob.at[slot], rb.at[slot], slot, 1, to)

    def copy_AJ(slot, to):
        return remote(oAJ.at[slot], rAJ.at[slot], slot, 2, to)

    def level(i, ahead):
        back = ahead // 2
        full = d >= ahead
        goes = d + ahead < devices

        @pl.when(d >= back)
        def _():
            J2, A2 = oAJ[i, N : 2 * N, :], oAJ[i, 0:N, :]
            S[:, N : 2 * N] = J2
            S[:, 2 * N : 3 * N] = A2.T
            T[:, N:] = B[...]

            @pl.when(i > 0)
            def _():
                copy_b(i, d).wait_recv()
                copy_L(i, d).wait_recv()

            b1 = rb[i]
            middle = rL[i] + J2
            S[:, 0:N] = middle
            T[:, 0:N] = middle + M[...]
            q = oAJ[i, 2 * N :, :] - dot(b1, J2, NT)
            S[:, 3 * N : 3 * N + 8] = q.T
            factor((T, 2), (S, 4))
            KB = T[:, N:]
            oL[i + 1] = oL[i] - dot(KB, KB, TN)

            @pl.when(goes)
            def _():
                copy_L(i + 1, d + ahead).start()

            ob[i + 1] = ob[i] + dot(b1, A2, NT) + dot(S[:, 3 * N : 3 * N + 8], S[:, 2 * N : 3 * N], TN)

        @pl.when(d < back)
        def _():
            oL[i + 1] = oL[i]
            ob[i + 1] = ob[i]

            @pl.when(goes)
            def _():
                copy_L(i + 1, d + ahead).start()

        @pl.when(goes)
        def _():
            copy_b(i + 1, d + ahead).start()

        @pl.when(full)
        def _():
            @pl.when(i > 0)
            def _():
                copy_AJ(i, d).wait_recv()

            A1, J2 = rAJ[i, 0:N, :], oAJ[i, N : 2 * N, :]
            q = oAJ[i, 2 * N :, :] - dot(rb[i], J2, NT)
            KR = dot(S[:, N : 2 * N], A1, NN)
            others = dot(jnp.concatenate([oAJ[i, 0 : 2 * N, :], q], axis=0), A1, NN)
            gram = dot(jnp.concatenate([KR, S[:, 2 * N :]], axis=1), KR, TN)
            moved = dot(A1, others[N : 2 * N, :], TN)
            A = others[0:N, :] - gram[N : 2 * N, :]
            oAJ[i + 1, 0:N, :] = A
            oAJ[i + 1, N : 2 * N, :] = rAJ[i, N : 2 * N, :] + moved - gram[0:N, :]
            oAJ[i + 1, 2 * N :, :] = (
                rAJ[i, 2 * N :, :] + others[2 * N :, :] - gram[2 * N : 2 * N + 8, :]
            )

            @pl.when(goes)
            def _():
                copy_AJ(i + 1, d + ahead).start()

            AL = dot(A, oL[i + 1], TN)
            B[...] = AL
            M[...] = dot(AL, A, NN)

        return ahead * 2

    lax.fori_loop(0, levels + 1, level, jnp.int32(1))

    g, z = gzs[0:1, :], gzs[2:3, :]
    S[:, 0:N] = oL[levels + 1] + jnp.where(eye, jnp.broadcast_to(g, (N, N)), 0.0)
    S[:, N : 2 * N] = unit
    S[:, 2 * N : 3 * N] = F.T
    factor((S.at[:, 0 : 3 * N], 3))
    K = S[:, 2 * N : 3 * N]
    pred = Q_ref[...] + dot(K, K, TN)
    K = S[:, N : 2 * N]
    cov = dot(K, K, TN)
    cov = 0.5 * (cov + cov.T)
    cov_ref[0] = cov
    mean = ob[levels + 1]
    mean = mean + dot(z - g * mean, cov, NN)
    mean_ref[0:1, :] = mean[0:1, :]
    g, z = gzs[1:2, :], gzs[3:4, :]
    across = jnp.broadcast_to(jnp.sqrt(g), (N, N))
    scaled = across.T * pred
    T[:, 0:N] = scaled * across + unit
    T[:, N:] = scaled
    factor((T, 2))
    K = T[:, N:]
    cov = pred - dot(K, K, TN)
    cov = 0.5 * (cov + cov.T)
    cov_ref[1] = cov
    mean = dot(mean, F, NT)
    mean = mean + dot(z - g * mean, cov, NN)
    mean_ref[1:2, :] = mean[0:1, :]

    @pl.when(d + 1 < devices)
    def _():
        gz_copy(d + 1).wait_send()

    def drain(i, ahead):
        @pl.when(d + ahead < devices)
        def _():
            copy_b(i + 1, d + ahead).wait_send()
            copy_L(i + 1, d + ahead).wait_send()

            @pl.when(d >= ahead)
            def _():
                copy_AJ(i + 1, d + ahead).wait_send()

        return ahead * 2

    lax.fori_loop(0, levels, drain, jnp.int32(1))


def local(outer, inner, obs, mask, smap, F, Q, r, pm, pv):
    devices = outer * inner
    levels = devices.bit_length() - 1
    vmem = pl.BlockSpec(memory_space=pltpu.VMEM)
    slots = levels + 2
    return pl.pallas_call(
        functools.partial(kernel, outer, inner),
        out_shape=(
            jax.ShapeDtypeStruct((2, N), F32),
            jax.ShapeDtypeStruct((2, N, N), F32),
        ),
        in_specs=[vmem] * 8,
        out_specs=(vmem, vmem),
        scratch_shapes=[
            pltpu.VMEM((slots, N, N), F32),
            pltpu.VMEM((slots, 8, N), F32),
            pltpu.VMEM((slots, 2 * N + 8, N), F32),
            pltpu.VMEM((slots, N, N), F32),
            pltpu.VMEM((slots, 8, N), F32),
            pltpu.VMEM((slots, 2 * N + 8, N), F32),
            pltpu.VMEM((N, N), F32),
            pltpu.VMEM((N, N), F32),
            pltpu.VMEM((N, 4 * N), F32),
            pltpu.VMEM((N, 2 * N), F32),
            pltpu.VMEM((8, N), F32),
            pltpu.VMEM((8, N), F32),
            pltpu.SemaphoreType.DMA((slots, 3)),
            pltpu.SemaphoreType.DMA((slots, 3)),
            pltpu.SemaphoreType.DMA((2,)),
        ],
        compiler_params=pltpu.CompilerParams(
            collective_id=0, has_side_effects=True, vmem_limit_bytes=48 * 1024 * 1024
        ),
    )(obs, mask, smap.reshape(1, N), F, Q, r.reshape(1, N), pm.reshape(1, N), pv.reshape(1, N))


def solution(mesh):
    outer, inner = mesh.shape["outer"], mesh.shape["inner"]
    split = P(("region", "outer", "inner"))
    return jax.shard_map(
        functools.partial(local, outer, inner),
        mesh=mesh,
        in_specs=(split, split, P("region"), P(), P(), P(), P("region"), P("region")),
        out_specs=(split, split),
        check_vma=False,
    )
```

time: 106 us -> 101 us (0.953)
  Pallas kernels: 101 us -> 96.7 us
    pallas_call x1, Pallas kernels: 101 us -> 96.7 us  [local(): pl.pallas_call(functools.partial(kernel, outer, inner), out_shape=(jax.Sh...]
where the time goes in v2:
time: 101 us
  Pallas kernels  96.7 us (96%)
  local copies, waits for them, and re-layouts  3.59 us (4%)
    pallas_call x1, Pallas kernels, local(): pl.pallas_call(functools.partial(kernel, outer, inner), out_shape=(jax.Sh...  96.7 us
    unnamed x18, local copies, waits for them, and re-layouts  3.59 us

profile of v2, /device:TPU:56, one launch (start us, length us, event | category | flops | bytes accessed | tf_op | source)
XLA Modules:
  0.0 101.0 jit_solution(13179670011141746686)
XLA Ops:
  0.6 0.0 copy-start.7
  0.6 0.0 copy-start.3
  0.7 0.0 copy-start.5
  0.7 0.0 copy-start.6
  0.7 0.0 copy-start.2
  0.7 0.0 copy-start.4
  0.7 0.6 copy-done.7
  1.3 0.0 copy-done.3
  1.3 0.0 copy-done.5
  1.3 0.0 copy-done.6
  1.3 0.0 copy-done.2
  1.4 0.0 copy-done.4
  1.4 0.0 copy-start
  1.4 0.8 copy-done
  2.2 0.0 copy-start.1
  2.2 0.8 copy-done.1
  3.1 96.7 %shard_map.95 = (f32[2,128]{1,0:T(2,128)S(1)}, f32[2,128,128]{2,1,0:T(8,128)S(1)}) custom-call(f32[2,128]{1,0:T(2,128)S(1)} %copy-done.2, s32[2,128]{1,0:T(2,128)S(1)} %copy-done.3, s32[1,128]{1,0:T(1,128)S(1)} %bitcast.4, f32[128,128]{1,0:T(8,128)S(1)} %copy-done, f32[128,128]{1,0:T(8,128)S(1)} %copy-done.1, f32[1,128]{1,0:T(1,128)S(1)} %bitcast.5, ...), custom_call_target="tpu_custom_call" | custom-call | tf_op jit(solution)/shard_map/pallas_call | solution.py:322
  99.8 0.6 copy.12
  100.4 0.7 copy.13
Async XLA Ops:
  0.6 0.7 copy-start.7
  0.6 0.7 copy-start.3
  0.7 0.7 copy-start.5
  0.7 0.7 copy-start.6
  0.7 0.7 copy-start.2
  0.7 0.7 copy-start.4
  1.4 0.8 copy-start
  2.2 0.8 copy-start.1
